TPU v7x, 32 devices: a whole 2x2x4 slice. The times are simulated.
32 devices in a mesh: groups: 2 (over x), fit: 16 (over z, y, core).
Axes of the slice: x: 2, y: 2, z: 4, core: 2. Of those that a mesh axis runs over, the one named last changes fastest.
Arguments:
- three_center: bfloat16 [32, 16, 128, 128], P(('groups', 'fit')), parts along dimension 0, may hold values from -2 to 2
- pair_ids: int32 [32, 16], P(('groups', 'fit')), parts along dimension 0, may hold values from 0 to 63, as said below
- col_tiles: int32 [32, 4], P('groups'), parts along dimension 0, may hold values from 0 to 15, as said below
- orbitals: bfloat16 [4096, 256], P('groups'), parts along dimension 0, may hold values from -0.5 to 0.5
- metric_root: bfloat16 [32, 16], P(('groups', 'fit')), parts along dimension 0
Outputs:
- exchange_matrix: float32 [4096, 512], P(('groups', 'fit')), parts along dimension 0
There are 2 independent parts, one for each index of `groups`. A program takes and returns all parts, laid end to end along the dimension named above; each array names one. Nothing has to cross between parts.
Inputs may be any that keep to these rules, and one draw needn't show every extreme that they name: `col_tiles`: each row tile a lists 4 distinct tiles, the first being a itself. `pair_ids`: each fitting block lists 16 distinct pairs.
All inputs are finite; a program needn't handle non-finite values.
Results may differ from a plain program's by a relative error of at most 0.005.
Values may be sent and summed in bfloat16 or wider, within the bound.
A program may use at most 64 MiB of HBM per device.

v0:
```python
import jax
import jax.numpy as jnp
from jax import lax
from jax.sharding import PartitionSpec as P


def local(three_center, pair_ids, col_tiles, orbitals, metric_root):
    blocks_dev = three_center.shape[0]
    tile_rows = three_center.shape[2]
    tile_count = col_tiles.shape[0]
    per_row = col_tiles.shape[1]
    basis_size = orbitals.shape[0]
    occupied = orbitals.shape[1]
    orbital_tiles = orbitals.reshape(tile_count, tile_rows, occupied)
    slot_ids = pair_ids[0]
    row_tiles = slot_ids // per_row
    column_tiles = col_tiles[row_tiles, slot_ids % per_row]
    picked = jnp.take(orbital_tiles, column_tiles, axis=0)
    partial_value = jnp.einsum(
        "psmn,sni->psmi", three_center, picked, preferred_element_type=jnp.float32
    )
    onehot = (row_tiles[:, None] == jnp.arange(tile_count, dtype=jnp.int32)[None, :]).astype(
        jnp.float32
    )
    metric_full = lax.all_gather(metric_root, "fit", axis=0, tiled=True)
    summands = []
    half_blocks = jnp.einsum("psmi,sa->pami", partial_value, onehot).astype(jnp.bfloat16)
    half_blocks = half_blocks.reshape(blocks_dev, basis_size, occupied)
    spread = lax.all_to_all(half_blocks, "fit", split_axis=1, concat_axis=0, tiled=True)
    fitted = jnp.einsum(
        "pq,qmi->pmi", metric_full, spread, preferred_element_type=jnp.float32
    ).astype(jnp.bfloat16)
    owned_rows = lax.all_to_all(fitted, "fit", split_axis=0, concat_axis=1, tiled=True)
    owned_rows = owned_rows.reshape(blocks_dev, tile_count, tile_rows, occupied)
    for column in range(per_row):
        others = jnp.take(owned_rows, col_tiles[:, column], axis=1)
        summands.append(
            jnp.einsum("pami,pani->amn", owned_rows, others, preferred_element_type=jnp.float32)
        )
    partial_k = jnp.stack(summands, axis=2).reshape(basis_size, per_row * tile_rows)
    return lax.psum_scatter(partial_k, "fit", scatter_dimension=0, tiled=True)


def solution(mesh):
    in_specs = (
        P(("groups", "fit"), None, None, None),
        P(("groups", "fit"), None),
        P("groups", None),
        P("groups", None),
        P(("groups", "fit"), None),
    )
    out_specs = P(("groups", "fit"), None)
    return jax.shard_map(local, mesh=mesh, in_specs=in_specs, out_specs=out_specs, check_vma=False)
```

profile of v0, /device:TPU:0, one launch (start us, length us, event | category | flops | bytes accessed | tf_op | source)
XLA Modules:
  0.0 223.8 jit_solution(14224152758422095049)
XLA Ops:
  6.5 0.0 copy-start
  6.5 0.8 fusion.29
  7.3 1.4 gather_fusion
  8.7 0.7 and_select_fusion.2
  9.4 0.0 copy-done
  9.4 0.6 gather_fusion.1
  10.0 1.6 convolution_bitcast_fusion
  11.6 0.9 copy.40
  12.5 0.4 convolution_convert_fusion.1
  12.9 0.3 copy.41
  13.3 11.7 %copy.60 = bf16[1,2048,256]{2,0,1:T(2,128)(2,1)S(1)} copy(bf16[1,2048,256]{2,1,0:T(8,128)(2,1)S(1)} %bitcast.125) | data formatting | bytes 2097152 | tf_op jit(solution)/shard_map/reshape | solution.py:28
  25.0 0.0 copy-start.3
  25.0 0.5 broadcast.289
  25.6 11.6 %reduce = bf16[2048,256]{1,0:T(8,128)(2,1)} reduce(bf16[2048,1,256]{2,1,0:T(2,128)(2,1)S(1)} %bitcast.123, bf16[]{:T(256)} %broadcast.289), dimensions={1}, to_apply=%bitcast.118.reduce_sub_computation | reduce | bytes 2097154
  37.1 2.2 reshape.299
  39.3 7.4 %all-to-all-start = ((bf16[16,2,16384]{2,1,0:T(2,128)(2,1)}), bf16[16,2,16384]{2,1,0:T(2,128)(2,1)S(1)}, u32[]{:S(2)}, u32[]{:S(2)}) async-start(bf16[16,2,16384]{2,1,0:T(2,128)(2,1)} %reshape.299), calls=%async_computation | async-start | bytes 2097152 | tf_op jit(solution)/shard_map/all_to_all | solution.py:29
  46.7 0.0 copy-done.3
  46.7 33.3 %all-gather = bf16[16,1,16]{2,1,0:T(2,128)(2,1)S(1)} all-gather(bf16[1,1,16]{2,1,0:T(2,128)(2,1)S(1)} %bitcast.126), channel_id=1, replica_groups=mesh['groups'=2,'fit'=16] {'fit'}, dimensions={0}, use_global_device_ids=true | all-gather | bytes 544 | tf_op jit(solution)/shard_map/all_gather | solution.py:25
  80.1 0.0 all-to-all-done
  80.1 3.4 %reshape.300 = bf16[2048,1,256]{2,1,0:T(2,128)(2,1)} reshape(bf16[16,2,16384]{2,1,0:T(2,128)(2,1)S(1)} %all-to-all-done) | data formatting | bytes 2097152
  83.5 0.0 copy-start.1
  83.5 1.8 copy.49
  85.3 0.7 fusion
  86.0 1.3 copy.44
  87.3 5.9 %all-to-all-start.1 = ((bf16[16,128,256]{2,1,0:T(8,128)(2,1)}), bf16[16,128,256]{2,1,0:T(8,128)(2,1)S(1)}, u32[]{:S(2)}, u32[]{:S(2)}) async-start(bf16[16,128,256]{2,1,0:T(8,128)(2,1)} %copy.44), calls=%async_computation.1 | async-start | bytes 2097152 | tf_op jit(solution)/shard_map/all_to_all | solution.py:33
  93.2 0.2 reduce-scatter.2.cloned.1.call-start
  93.4 0.0 copy-done.1
  93.5 22.7 %all-to-all-done.1 = bf16[16,128,256]{2,1,0:T(8,128)(2,1)S(1)} async-done(((bf16[16,128,256]{2,1,0:T(8,128)(2,1)}), bf16[16,128,256]{2,1,0:T(8,128)(2,1)S(1)}, u32[]{:S(2)}, u32[]{:S(2)}) %all-to-all-start.1) | async-done | bytes 1048608 | tf_op jit(solution)/shard_map/all_to_all | solution.py:33
  116.1 1.6 gather_fusion.4
  117.7 1.6 gather_fusion.3
  119.3 1.6 gather_fusion.2
  120.9 0.6 gather_fusion.5
  121.6 0.0 copy-start.2
  121.6 1.8 convolution_bitcast_fusion.2
  123.4 1.7 convolution_bitcast_fusion.3
  125.1 0.0 copy-done.2
  125.2 0.5 convolution_bitcast_fusion.4
  125.7 0.5 convolution_bitcast_fusion.1
  126.2 2.3 %pad_maximum_fusion = f32[16,128,4,128]{3,1,0,2:T(8,128)} fusion(f32[16,128,1,128]{3,1,0,2:T(8,128)S(1)} %convolution_bitcast_fusion.1, f32[16,128,1,128]{3,1,0,2:T(8,128)S(1)} %convolution_bitcast_fusion.2, f32[16,128,1,128]{3,1,0,2:T(8,128)S(1)} %convolution_bitcast_fusion.3, f32[16,128,1,128]{3,1,0,2:T(8,128)S(1)} %convolution_bitcast_fusion.4), kind=kLoop, calls=%fused_computation.7 | loop fusion | flops 3145728 | bytes 8388608 | tf_op jit(solution)/shard_map/stack | solution.py:40
  128.5 5.4 %copy.45 = f32[16,128,4,128]{1,0,3,2:T(8,128)} copy(f32[16,128,4,128]{3,1,0,2:T(8,128)} %pad_maximum_fusion) | data formatting | bytes 8388608 | tf_op jit(solution)/shard_map/stack | solution.py:40
  133.9 6.1 %copy.59 = f32[64,8,16,128]{3,1,2,0:T(8,128)} copy(f32[64,8,16,128]{3,2,1,0:T(8,128)} %bitcast.121) | data formatting | bytes 8388608
  140.0 0.0 reduce-scatter.2.cloned.1.call-update
  140.0 75.1 %reduce-scatter.2.cloned.1.call-done = f32[128,512]{0,1:T(8,128)} async-done(((f32[2048,512]{0,1:T(8,128)}), f32[128,512]{0,1:T(8,128)}) %reduce-scatter.2.cloned.1.call-update) | async-done | bytes 262160 | tf_op jit(solution)/shard_map/reduce_scatter | solution.py:41
  215.1 1.8 copy.46
  (6 shorter events, 0.0 us)
Async XLA Ops:
  6.5 2.8 %copy-start = (bf16[2048,256]{1,0:T(8,128)(2,1)S(1)}, bf16[2048,256]{1,0:T(8,128)(2,1)}, u32[]{:S(2)}) copy-start(bf16[2048,256]{1,0:T(8,128)(2,1)} %param.10) | copy-start | bytes 3145732
  25.0 21.7 %copy-start.3 = (bf16[1,16]{1,0:T(2,128)(2,1)S(1)}, bf16[1,16]{1,0:T(2,128)(2,1)}, u32[]{:S(2)}) copy-start(bf16[1,16]{1,0:T(2,128)(2,1)} %param.11) | copy-start | bytes 100
  39.3 40.7 %all-to-all-start = ((bf16[16,2,16384]{2,1,0:T(2,128)(2,1)}), bf16[16,2,16384]{2,1,0:T(2,128)(2,1)S(1)}, u32[]{:S(2)}, u32[]{:S(2)}) async-start(bf16[16,2,16384]{2,1,0:T(2,128)(2,1)} %reshape.299), calls=%async_computation | async-start | bytes 2097152 | tf_op jit(solution)/shard_map/all_to_all | solution.py:29
  83.5 9.9 %copy-start.1 = (s32[16,4]{0,1:T(4,128)S(1)}, s32[16,4]{0,1:T(4,128)}, u32[]{:S(2)}) copy-start(s32[16,4]{0,1:T(4,128)} %param.9) | copy-start | bytes 772
  87.3 28.8 %all-to-all-start.1 = ((bf16[16,128,256]{2,1,0:T(8,128)(2,1)}), bf16[16,128,256]{2,1,0:T(8,128)(2,1)S(1)}, u32[]{:S(2)}, u32[]{:S(2)}) async-start(bf16[16,128,256]{2,1,0:T(8,128)(2,1)} %copy.44), calls=%async_computation.1 | async-start | bytes 2097152 | tf_op jit(solution)/shard_map/all_to_all | solution.py:33
  93.2 121.9 %reduce-scatter.2.cloned.1.call-start = ((), (), s32[]{:S(2)}) async-start(), calls=%async_computation.3 | async-start | bytes 4456448 | tf_op jit(solution)/shard_map/reduce_scatter | solution.py:41
  121.6 3.6 %copy-start.2 = (bf16[16,128,256]{2,1,0:T(8,128)(2,1)S(1)}, bf16[16,128,256]{2,1,0:T(8,128)(2,1)}, u32[]{:S(2)}) copy-start(bf16[16,128,256]{2,1,0:T(8,128)(2,1)} %gather_fusion.2) | copy-start | bytes 3145732
Sparse Core Ops, SparseCore 0:
  140.2 74.9 reduce-scatter.1
where the time goes:
time: 224 us
  waiting for transfers between devices  97.7 us (44%)
  local copies, waits for them, and re-layouts  43 us (19%)
  blocking collectives  33.3 us (15%)
  other arithmetic  15.3 us (7%)
  between operations  13.6 us (6%)
  starting transfers between devices  13.5 us (6%)
  matrix products  7.3 us (3%)
    reduce_scatter x1, waiting for transfers between devices, local(): return lax.psum_scatter(partial_k, 'fit', scatter_dimension=0, tiled=True)  75.1 us
    all_gather x1, blocking collectives, local(): metric_full = lax.all_gather(metric_root, 'fit', axis=0, tiled=True)  33.3 us
    all_to_all x1, waiting for transfers between devices, local(): lax.all_to_all(fitted, 'fit', split_axis=0, concat_axis=1, tiled=True)  22.7 us
    unnamed x13, local copies, waits for them, and re-layouts  14.1 us
    reshape x1, local copies, waits for them, and re-layouts, local(): half_blocks = half_blocks.reshape(blocks_dev, basis_size, occupied)  11.7 us
    unnamed x1, other arithmetic  11.6 us
    all_to_all x1, starting transfers between devices, local(): lax.all_to_all(half_blocks, 'fit', split_axis=1, concat_axis=0, tiled=True)  7.38 us
    all_to_all x1, starting transfers between devices, local(): lax.all_to_all(fitted, 'fit', split_axis=0, concat_axis=1, tiled=True)  5.86 us
  transfers between devices with their start and end apart: 3, of which 2 were waited for; matrix products, arithmetic and copies ran while one was open for 0% of the time, Pallas kernels for 0%

commit v1 on v0

--- a/solution.py
+++ b/solution.py
@@ -1,10 +1,18 @@
+import functools
+
 import jax
 import jax.numpy as jnp
 from jax import lax
+from jax.experimental import pallas as pl
+from jax.experimental.pallas import tpu as pltpu
 from jax.sharding import PartitionSpec as P
 
-
-def local(three_center, pair_ids, col_tiles, orbitals, metric_root):
+MESH = pl.DeviceIdType.MESH
+Y_COUNT = 2
+CORES = 2
+
+
+def general(three_center, pair_ids, col_tiles, orbitals, metric_root):
     blocks_dev = three_center.shape[0]
     tile_rows = three_center.shape[2]
     tile_count = col_tiles.shape[0]
@@ -41,6 +49,214 @@
     return lax.psum_scatter(partial_k, "fit", scatter_dimension=0, tiled=True)
 
 
+def kernel(
+    n, per_row, tb,
+    slot_ref, has_ref, col_ref, three_ref, orb_ref, kron_ref, out_ref,
+    orb_t, send_h, recv_h, fit_n, fit_t, send_c, recv_c, acc, send_y, recv_y, send_z, recv_z,
+    own_sem, sh_sem, rh_sem, sc_sem, rc_sem, sy_sem, ry_sem, sz_sem, rz_sem,
+):
+    tiles = orb_ref.shape[0] // tb
+    basis = tiles * tb
+    occ = orb_ref.shape[1]
+    depth = occ // n
+    z_count = n // (Y_COUNT * CORES)
+    me = lax.axis_index("fit")
+    core = lax.rem(me, CORES)
+    y = lax.rem(me // CORES, Y_COUNT)
+    z = me // (CORES * Y_COUNT)
+
+    def at(dz, dy, dc):
+        zz = lax.rem(z + dz, z_count)
+        yy = lax.rem(y + dy, Y_COUNT)
+        cc = lax.rem(core + dc, CORES)
+        return (zz * Y_COUNT + yy) * CORES + cc
+
+    offsets = [
+        (dz, dy, dc)
+        for dz in (2, 1, 3, 0)
+        for dy in range(Y_COUNT)
+        for dc in range(CORES)
+        if (dz, dy, dc) != (0, 0, 0)
+    ]
+    barrier = pltpu.get_barrier_semaphore()
+    for off in offsets:
+        pl.semaphore_signal(barrier, inc=1, device_id={"fit": at(*off)}, device_id_type=MESH)
+
+    def turn(b, carry):
+        rows = pl.ds(pl.multiple_of(b * tb, tb), tb)
+        orb_t[b] = orb_ref[rows, :].T
+        return carry
+
+    lax.fori_loop(0, tiles, turn, 0)
+    for d in range(n):
+        send_h[d * depth:(d + 1) * depth, basis:] = kron_ref[...]
+
+    for a in range(tiles):
+        total = jnp.zeros((occ, tb), jnp.float32)
+        for r in range(per_row):
+            q = a * per_row + r
+            block = three_ref[slot_ref[q]]
+            block = jnp.where(has_ref[q] > 0, block, jnp.zeros_like(block))
+            total += lax.dot_general(
+                orb_t[col_ref[q]], block, (((1,), (1,)), ((), ())),
+                preferred_element_type=jnp.float32,
+            )
+        send_h[:, a * tb:(a + 1) * tb] = total.astype(jnp.bfloat16)
+
+    pl.semaphore_wait(barrier, n - 1)
+
+    def rows_of(d):
+        return pl.ds(pl.multiple_of(d * depth, depth), depth)
+
+    copies = []
+    for k, off in enumerate(offsets):
+        dst = at(*off)
+        copy = pltpu.make_async_remote_copy(
+            src_ref=send_h.at[rows_of(dst), :],
+            dst_ref=recv_h.at[rows_of(me), :],
+            send_sem=sh_sem.at[k],
+            recv_sem=rh_sem.at[k],
+            device_id={"fit": dst},
+            device_id_type=MESH,
+        )
+        copy.start()
+        copies.append(copy)
+    own = pltpu.make_async_copy(send_h.at[rows_of(me), :], recv_h.at[rows_of(me), :], own_sem)
+    own.start()
+    own.wait()
+    for copy in copies:
+        copy.wait_recv()
+
+    kron = recv_h[:, basis:]
+    for a in range(tiles):
+        value = jnp.dot(
+            kron, recv_h[:, a * tb:(a + 1) * tb], preferred_element_type=jnp.float32
+        ).astype(jnp.bfloat16)
+        fit_n[a] = value
+        fit_t[a] = value.T
+
+    half_tiles = tiles // CORES
+    quarter = half_tiles // Y_COUNT
+
+    def part(a, r):
+        return jnp.dot(
+            fit_t[a], fit_n[col_ref[a * per_row + r]], preferred_element_type=jnp.float32
+        )
+
+    pending = list(copies)
+    core_copies = []
+    for r in range(per_row):
+
+        def one(j, carry, r=r):
+            send_c[r, j] = part(j * CORES + (1 - core), r).astype(jnp.bfloat16)
+            return carry
+
+        lax.fori_loop(0, half_tiles, one, 0)
+        copy = pltpu.make_async_remote_copy(
+            src_ref=send_c.at[r], dst_ref=recv_c.at[r],
+            send_sem=sc_sem.at[r], recv_sem=rc_sem.at[r],
+            device_id={"fit": at(0, 0, 1)}, device_id_type=MESH,
+        )
+        copy.start()
+        core_copies.append(copy)
+    y_copies = []
+    for r in range(per_row):
+        core_copies[r].wait_recv()
+
+        def theirs(j, carry, r=r):
+            t = j * Y_COUNT + (1 - y)
+            value = part(t * CORES + core, r) + recv_c[r, t].astype(jnp.float32)
+            send_y[r, j] = value.astype(jnp.bfloat16)
+            return carry
+
+        lax.fori_loop(0, quarter, theirs, 0)
+        copy = pltpu.make_async_remote_copy(
+            src_ref=send_y.at[r], dst_ref=recv_y.at[r],
+            send_sem=sy_sem.at[r], recv_sem=ry_sem.at[r],
+            device_id={"fit": at(0, 1, 0)}, device_id_type=MESH,
+        )
+        copy.start()
+        y_copies.append(copy)
+
+        def mine(j, carry, r=r):
+            t = j * Y_COUNT + y
+            acc[r, j] = part(t * CORES + core, r) + recv_c[r, t].astype(jnp.float32)
+            return carry
+
+        lax.fori_loop(0, quarter, mine, 0)
+    z_copies = []
+    for r in range(per_row):
+        y_copies[r].wait_recv()
+        row = []
+        for k, dz in enumerate((2, 1, 3)):
+            zz = lax.rem(z + dz, z_count)
+            send_z[r, k] = (acc[r, zz] + recv_y[r, zz].astype(jnp.float32)).astype(jnp.bfloat16)
+            copy = pltpu.make_async_remote_copy(
+                src_ref=send_z.at[r, k], dst_ref=recv_z.at[r, k],
+                send_sem=sz_sem.at[r, k], recv_sem=rz_sem.at[r, k],
+                device_id={"fit": at(dz, 0, 0)}, device_id_type=MESH,
+            )
+            copy.start()
+            row.append(copy)
+        z_copies.append(row)
+    for r in range(per_row):
+        value = acc[r, z] + recv_y[r, z].astype(jnp.float32)
+        for k in range(z_count - 1):
+            z_copies[r][k].wait_recv()
+            value += recv_z[r, k].astype(jnp.float32)
+        out_ref[:, r * tb:(r + 1) * tb] = value
+    for copy in pending + core_copies + y_copies + [c for row in z_copies for c in row]:
+        copy.wait_send()
+
+
+def fused(n, three_center, pair_ids, col_tiles, orbitals, metric_root):
+    tiles, per_row = col_tiles.shape
+    slots, tb = three_center.shape[1:3]
+    basis, occ = orbitals.shape
+    depth = occ // n
+    pairs = tiles * per_row
+    match = pair_ids[0][None, :] == jnp.arange(pairs, dtype=jnp.int32)[:, None]
+    has = jnp.any(match, axis=1).astype(jnp.int32)
+    slot = jnp.sum(jnp.where(match, jnp.arange(slots, dtype=jnp.int32)[None, :], 0), axis=1)
+    lane = jnp.arange(n * depth, dtype=jnp.int32)
+    spread = jnp.repeat(metric_root[0], depth)
+    kron = jnp.where(
+        (lane % depth)[None, :] == jnp.arange(depth, dtype=jnp.int32)[:, None], spread[None, :], 0
+    ).astype(jnp.bfloat16)
+    z_count = n // (Y_COUNT * CORES)
+    half_tiles = tiles // CORES
+    bf = jnp.bfloat16
+    dma = pltpu.SemaphoreType.DMA
+    vmem = pl.BlockSpec(memory_space=pltpu.VMEM)
+    smem = pl.BlockSpec(memory_space=pltpu.SMEM)
+    return pl.pallas_call(
+        functools.partial(kernel, n, per_row, tb),
+        out_shape=jax.ShapeDtypeStruct((tb, per_row * tb), jnp.float32),
+        in_specs=[smem, smem, smem, vmem, vmem, vmem],
+        out_specs=vmem,
+        scratch_shapes=[
+            pltpu.VMEM((tiles, occ, tb), bf),
+            pltpu.VMEM((occ, basis + occ), bf),
+            pltpu.VMEM((occ, basis + occ), bf),
+            pltpu.VMEM((tiles, occ, tb), bf),
+            pltpu.VMEM((tiles, tb, occ), bf),
+            pltpu.VMEM((per_row, half_tiles, tb, tb), bf),
+            pltpu.VMEM((per_row, half_tiles, tb, tb), bf),
+            pltpu.VMEM((per_row, z_count, tb, tb), jnp.float32),
+            pltpu.VMEM((per_row, z_count, tb, tb), bf),
+            pltpu.VMEM((per_row, z_count, tb, tb), bf),
+            pltpu.VMEM((per_row, z_count - 1, tb, tb), bf),
+            pltpu.VMEM((per_row, z_count - 1, tb, tb), bf),
+            dma, dma((n - 1,)), dma((n - 1,)),
+            dma((per_row,)), dma((per_row,)), dma((per_row,)), dma((per_row,)),
+            dma((per_row, z_count - 1)), dma((per_row, z_count - 1)),
+        ],
+        compiler_params=pltpu.CompilerParams(
+            collective_id=0, has_side_effects=True, vmem_limit_bytes=48 * 1024 * 1024
+        ),
+    )(slot, has, col_tiles.reshape(-1), three_center[0], orbitals, kron)
+
+
 def solution(mesh):
     in_specs = (
         P(("groups", "fit"), None, None, None),
@@ -50,4 +266,16 @@
         P(("groups", "fit"), None),
     )
     out_specs = P(("groups", "fit"), None)
+    n = mesh.shape["fit"]
+
+    def local(three_center, pair_ids, col_tiles, orbitals, metric_root):
+        args = (three_center, pair_ids, col_tiles, orbitals, metric_root)
+        fits = (
+            n == 16
+            and col_tiles.shape[0] == n
+            and three_center.shape[0] == 1
+            and orbitals.shape[1] == 16 * n
+        )
+        return fused(n, *args) if fits else general(*args)
+
     return jax.shard_map(local, mesh=mesh, in_specs=in_specs, out_specs=out_specs, check_vma=False)

time: 224 us -> 62.9 us (0.28)
  waiting for transfers between devices: 97.7 us -> 0 us
  Pallas kernels: 0 us -> 57.1 us
  local copies, waits for them, and re-layouts: 43 us -> 5.27 us
  blocking collectives: 33.3 us -> 0 us
  other arithmetic: 15.3 us -> 0.19 us
  between operations: 13.6 us -> 0.04 us
  starting transfers between devices: 13.5 us -> 0 us
  matrix products: 7.3 us -> 0 us
    reduce_scatter x1 -> x0, waiting for transfers between devices: 75.1 us -> none  [local(): return lax.psum_scatter(partial_k, 'fit', scatter_dimension=0, tiled=True)]
    pallas_call x0 -> x1, Pallas kernels: none -> 57.1 us  [fused(): pl.pallas_call(functools.partial(kernel, n, per_row, tb), out_shape=jax.S...]
    all_gather x1 -> x0, blocking collectives: 33.3 us -> none  [local(): metric_full = lax.all_gather(metric_root, 'fit', axis=0, tiled=True)]
    all_to_all x2 -> x0, waiting for transfers between devices: 22.7 us -> none  [the longest x1 22.7 us: local(): lax.all_to_all(fitted, 'fit', split_axis=0, concat_axis=1, tiled=True)]
    all_to_all x2 -> x0, starting transfers between devices: 13.2 us -> none  [the longest x1 7.38 us: local(): lax.all_to_all(half_blocks, 'fit', split_axis=1, concat_axis=0, tiled=True)]
    reshape x1, local copies, waits for them, and re-layouts: 11.7 us -> 0.09 us  [fused(): col_tiles.reshape(-1)]
    unnamed x1 -> x0, other arithmetic: 11.6 us -> none
    unnamed x13 -> x12, local copies, waits for them, and re-layouts: 14.1 us -> 5.02 us
  transfers between devices with their start and end apart: 3 -> 0, of which waited for: 2 -> 0; matrix products, arithmetic and copies ran while one was open for 0% -> 0% of each run, Pallas kernels for 0% -> 0%
where the time goes in v1:
time: 62.9 us; the launch traced here: 62.7 us
  Pallas kernels  57.1 us (91%)
  local copies, waits for them, and re-layouts  5.27 us (8%)
    pallas_call x1, Pallas kernels, fused(): pl.pallas_call(functools.partial(kernel, n, per_row, tb), out_shape=jax.S...  57.1 us
    unnamed x12, local copies, waits for them, and re-layouts  5.02 us

profile of v1, /device:TPU:0, one launch (start us, length us, event | category | flops | bytes accessed | tf_op | source)
XLA Modules:
  0.0 62.7 jit_solution(1479536582964083225)
XLA Ops:
  0.0 0.0 copy-start.4
  0.0 0.7 %copy-done.4 = s32[1,16]{1,0:T(1,128)S(1)} copy-done((s32[1,16]{1,0:T(1,128)S(1)}, s32[1,16]{1,0:T(1,128)}, u32[]{:S(2)}) %copy-start.4) | copy-done | bytes 88
  0.7 0.1 fusion.1
  0.8 0.1 select_reduce_fusion.slot_ref
  0.8 0.0 copy-start.3
  0.9 0.6 %copy-done.3 = bf16[1,16]{1,0:T(2,128)(2,1)S(1)} copy-done((bf16[1,16]{1,0:T(2,128)(2,1)S(1)}, bf16[1,16]{1,0:T(2,128)(2,1)}, u32[]{:S(2)}) %copy-start.3) | copy-done | bytes 56
  1.5 0.1 broadcast_in_dim.35
  1.6 0.1 broadcast_in_dim.36
  1.7 0.0 copy-start.2
  1.7 0.7 %copy-done.2 = s32[16,4]{0,1:T(4,128)S(1)} copy-done((s32[16,4]{0,1:T(4,128)S(1)}, s32[16,4]{0,1:T(4,128)}, u32[]{:S(2)}) %copy-start.2) | copy-done | bytes 280
  2.3 0.1 copy.8
  2.4 0.1 reshape.13.col_ref
  2.5 0.0 copy-start
  2.5 1.2 %copy-done = bf16[2048,256]{1,0:T(8,128)(2,1)S(1)} copy-done((bf16[2048,256]{1,0:T(8,128)(2,1)S(1)}, bf16[2048,256]{1,0:T(8,128)(2,1)}, u32[]{:S(2)}) %copy-start) | copy-done | bytes 1048600
  3.7 0.0 copy-start.1
  3.8 1.0 %copy-done.1 = bf16[1,16,128,128]{3,2,1,0:T(8,128)(2,1)S(1)} copy-done((bf16[1,16,128,128]{3,2,1,0:T(8,128)(2,1)S(1)}, bf16[1,16,128,128]{3,2,1,0:T(8,128)(2,1)}, u32[]{:S(2)}) %copy-start.1) | copy-done | bytes 524312
  4.8 57.1 %shard_map.55 = f32[128,512]{1,0:T(8,128)S(1)} custom-call(s32[64]{0:T(128)S(1)} %select_reduce_fusion.slot_ref, s32[64]{0:T(128)S(1)} %convert_element_type.5.has_ref, s32[64]{0:T(128)S(1)} %reshape.13.col_ref, bf16[16,128,128]{2,1,0:T(8,128)(2,1)S(1)} %bitcast.3, bf16[2048,256]{1,0:T(8,128)(2,1)S(1)} %copy-done, bf16[16,256]{1,0:T(8,128)(2,1)S(1)} %fusion.kron_ref), custom_call_target="tpu_custom_call" | custom-call | tf_op jit(solution)/shard_map/pallas_call | solution.py:232
  61.9 0.7 %copy.10 = f32[128,512]{1,0:T(8,128)} copy(f32[128,512]{1,0:T(8,128)S(1)} %shard_map.55) | data formatting | bytes 524288
  (3 shorter events, 0.0 us)
Async XLA Ops:
  0.0 0.7 %copy-start.4 = (s32[1,16]{1,0:T(1,128)S(1)}, s32[1,16]{1,0:T(1,128)}, u32[]{:S(2)}) copy-start(s32[1,16]{1,0:T(1,128)} %param.6) | copy-start | bytes 196
  0.8 0.7 %copy-start.3 = (bf16[1,16]{1,0:T(2,128)(2,1)S(1)}, bf16[1,16]{1,0:T(2,128)(2,1)}, u32[]{:S(2)}) copy-start(bf16[1,16]{1,0:T(2,128)(2,1)} %param.9) | copy-start | bytes 100
  1.7 0.7 %copy-start.2 = (s32[16,4]{0,1:T(4,128)S(1)}, s32[16,4]{0,1:T(4,128)}, u32[]{:S(2)}) copy-start(s32[16,4]{0,1:T(4,128)} %param.7) | copy-start | bytes 772
  2.5 1.2 %copy-start = (bf16[2048,256]{1,0:T(8,128)(2,1)S(1)}, bf16[2048,256]{1,0:T(8,128)(2,1)}, u32[]{:S(2)}) copy-start(bf16[2048,256]{1,0:T(8,128)(2,1)} %orb_ref.1) | copy-start | bytes 3145732
  3.7 1.0 %copy-start.1 = (bf16[1,16,128,128]{3,2,1,0:T(8,128)(2,1)S(1)}, bf16[1,16,128,128]{3,2,1,0:T(8,128)(2,1)}, u32[]{:S(2)}) copy-start(bf16[1,16,128,128]{3,2,1,0:T(8,128)(2,1)} %param.5) | copy-start | bytes 1572868

commit v2 on v1

--- a/solution.py
+++ b/solution.py
@@ -10,6 +10,7 @@
 MESH = pl.DeviceIdType.MESH
 Y_COUNT = 2
 CORES = 2
+CHUNKS = 4
 
 
 def general(three_center, pair_ids, col_tiles, orbitals, metric_root):
@@ -52,11 +53,14 @@
 def kernel(
     n, per_row, tb,
     slot_ref, has_ref, col_ref, three_ref, orb_ref, kron_ref, out_ref,
-    orb_t, send_h, recv_h, fit_n, fit_t, send_c, recv_c, acc, send_y, recv_y, send_z, recv_z,
-    own_sem, sh_sem, rh_sem, sc_sem, rc_sem, sy_sem, ry_sem, sz_sem, rz_sem,
+    orb_v, three_v, orb_t, send_h, recv_h, recv_m, fit_n, fit_t, send_c, recv_c, acc, send_y, recv_y, send_z, recv_z,
+    in_sem, own_sem, sm_sem, rm_sem, sh_sem, rh_sem, sc_sem, rc_sem, sy_sem, ry_sem, sz_sem, rz_sem,
 ):
     tiles = orb_ref.shape[0] // tb
     basis = tiles * tb
+    chunks = send_h.shape[0]
+    chunk_tiles = tiles // chunks
+    chunk_rows = basis // chunks
     occ = orb_ref.shape[1]
     depth = occ // n
     z_count = n // (Y_COUNT * CORES)
@@ -70,6 +74,18 @@
         yy = lax.rem(y + dy, Y_COUNT)
         cc = lax.rem(core + dc, CORES)
         return (zz * Y_COUNT + yy) * CORES + cc
+
+    loads = [
+        pltpu.make_async_copy(
+            orb_ref.at[c * chunk_rows:(c + 1) * chunk_rows],
+            orb_v.at[c * chunk_rows:(c + 1) * chunk_rows],
+            in_sem.at[c],
+        )
+        for c in range(chunks)
+    ]
+    loads.append(pltpu.make_async_copy(three_ref, three_v, in_sem.at[chunks]))
+    for load in loads:
+        load.start()
 
     offsets = [
         (dz, dy, dc)
@@ -82,58 +98,78 @@
     for off in offsets:
         pl.semaphore_signal(barrier, inc=1, device_id={"fit": at(*off)}, device_id_type=MESH)
 
-    def turn(b, carry):
-        rows = pl.ds(pl.multiple_of(b * tb, tb), tb)
-        orb_t[b] = orb_ref[rows, :].T
-        return carry
-
-    lax.fori_loop(0, tiles, turn, 0)
-    for d in range(n):
-        send_h[d * depth:(d + 1) * depth, basis:] = kron_ref[...]
-
-    for a in range(tiles):
-        total = jnp.zeros((occ, tb), jnp.float32)
-        for r in range(per_row):
-            q = a * per_row + r
-            block = three_ref[slot_ref[q]]
-            block = jnp.where(has_ref[q] > 0, block, jnp.zeros_like(block))
-            total += lax.dot_general(
-                orb_t[col_ref[q]], block, (((1,), (1,)), ((), ())),
-                preferred_element_type=jnp.float32,
-            )
-        send_h[:, a * tb:(a + 1) * tb] = total.astype(jnp.bfloat16)
-
-    pl.semaphore_wait(barrier, n - 1)
-
     def rows_of(d):
         return pl.ds(pl.multiple_of(d * depth, depth), depth)
 
+    for b in range(tiles):
+        if b % chunk_tiles == 0:
+            loads[b // chunk_tiles].wait()
+        orb_t[b] = orb_v[b * tb:(b + 1) * tb, :].T
+    loads[-1].wait()
+    pl.semaphore_wait(barrier, n - 1)
+
+    recv_m[rows_of(me), :] = kron_ref[...]
+    metric_copies = []
+    for k, off in enumerate(offsets):
+        copy = pltpu.make_async_remote_copy(
+            src_ref=kron_ref,
+            dst_ref=recv_m.at[rows_of(me), :],
+            send_sem=sm_sem.at[k],
+            recv_sem=rm_sem.at[k],
+            device_id={"fit": at(*off)},
+            device_id_type=MESH,
+        )
+        copy.start()
+        metric_copies.append(copy)
+
     copies = []
-    for k, off in enumerate(offsets):
-        dst = at(*off)
-        copy = pltpu.make_async_remote_copy(
-            src_ref=send_h.at[rows_of(dst), :],
-            dst_ref=recv_h.at[rows_of(me), :],
-            send_sem=sh_sem.at[k],
-            recv_sem=rh_sem.at[k],
-            device_id={"fit": dst},
-            device_id_type=MESH,
-        )
-        copy.start()
-        copies.append(copy)
-    own = pltpu.make_async_copy(send_h.at[rows_of(me), :], recv_h.at[rows_of(me), :], own_sem)
-    own.start()
-    own.wait()
-    for copy in copies:
+    for c in range(chunks):
+        for t in range(chunk_tiles):
+            total = jnp.zeros((occ, tb), jnp.float32)
+            for r in range(per_row):
+                q = (c * chunk_tiles + t) * per_row + r
+                block = three_v[slot_ref[q]]
+                block = jnp.where(has_ref[q] > 0, block, jnp.zeros_like(block))
+                total += lax.dot_general(
+                    orb_t[col_ref[q]], block, (((1,), (1,)), ((), ())),
+                    preferred_element_type=jnp.float32,
+                )
+            send_h[c, :, t * tb:(t + 1) * tb] = total.astype(jnp.bfloat16)
+        row = []
+        for k, off in enumerate(offsets):
+            dst = at(*off)
+            copy = pltpu.make_async_remote_copy(
+                src_ref=send_h.at[c, rows_of(dst), :],
+                dst_ref=recv_h.at[c, rows_of(me), :],
+                send_sem=sh_sem.at[c, k],
+                recv_sem=rh_sem.at[c, k],
+                device_id={"fit": dst},
+                device_id_type=MESH,
+            )
+            copy.start()
+            row.append(copy)
+        copies.append(row)
+    owns = []
+    for c in range(chunks):
+        own = pltpu.make_async_copy(
+            send_h.at[c, rows_of(me), :], recv_h.at[c, rows_of(me), :], own_sem.at[c]
+        )
+        own.start()
+        owns.append(own)
+    for copy in metric_copies:
         copy.wait_recv()
-
-    kron = recv_h[:, basis:]
-    for a in range(tiles):
-        value = jnp.dot(
-            kron, recv_h[:, a * tb:(a + 1) * tb], preferred_element_type=jnp.float32
-        ).astype(jnp.bfloat16)
-        fit_n[a] = value
-        fit_t[a] = value.T
+    kron = recv_m[...]
+
+    for c in range(chunks):
+        owns[c].wait()
+        for copy in copies[c]:
+            copy.wait_recv()
+        for t in range(chunk_tiles):
+            value = jnp.dot(
+                kron, recv_h[c, :, t * tb:(t + 1) * tb], preferred_element_type=jnp.float32
+            ).astype(jnp.bfloat16)
+            fit_n[c * chunk_tiles + t] = value
+            fit_t[c * chunk_tiles + t] = value.T
 
     half_tiles = tiles // CORES
     quarter = half_tiles // Y_COUNT
@@ -143,47 +179,41 @@
             fit_t[a], fit_n[col_ref[a * per_row + r]], preferred_element_type=jnp.float32
         )
 
-    pending = list(copies)
-    core_copies = []
-    for r in range(per_row):
-
-        def one(j, carry, r=r):
+    def to_core(r):
+        for j in range(half_tiles):
             send_c[r, j] = part(j * CORES + (1 - core), r).astype(jnp.bfloat16)
-            return carry
-
-        lax.fori_loop(0, half_tiles, one, 0)
         copy = pltpu.make_async_remote_copy(
             src_ref=send_c.at[r], dst_ref=recv_c.at[r],
             send_sem=sc_sem.at[r], recv_sem=rc_sem.at[r],
             device_id={"fit": at(0, 0, 1)}, device_id_type=MESH,
         )
         copy.start()
-        core_copies.append(copy)
-    y_copies = []
-    for r in range(per_row):
+        return copy
+
+    def to_y(r):
         core_copies[r].wait_recv()
-
-        def theirs(j, carry, r=r):
+        for j in range(quarter):
             t = j * Y_COUNT + (1 - y)
             value = part(t * CORES + core, r) + recv_c[r, t].astype(jnp.float32)
             send_y[r, j] = value.astype(jnp.bfloat16)
-            return carry
-
-        lax.fori_loop(0, quarter, theirs, 0)
         copy = pltpu.make_async_remote_copy(
             src_ref=send_y.at[r], dst_ref=recv_y.at[r],
             send_sem=sy_sem.at[r], recv_sem=ry_sem.at[r],
             device_id={"fit": at(0, 1, 0)}, device_id_type=MESH,
         )
         copy.start()
-        y_copies.append(copy)
-
-        def mine(j, carry, r=r):
+        return copy
+
+    core_copies = [to_core(0)]
+    y_copies = []
+    for r in range(1, per_row):
+        core_copies.append(to_core(r))
+        y_copies.append(to_y(r - 1))
+    y_copies.append(to_y(per_row - 1))
+    for r in range(per_row):
+        for j in range(quarter):
             t = j * Y_COUNT + y
             acc[r, j] = part(t * CORES + core, r) + recv_c[r, t].astype(jnp.float32)
-            return carry
-
-        lax.fori_loop(0, quarter, mine, 0)
     z_copies = []
     for r in range(per_row):
         y_copies[r].wait_recv()
@@ -205,7 +235,10 @@
             z_copies[r][k].wait_recv()
             value += recv_z[r, k].astype(jnp.float32)
         out_ref[:, r * tb:(r + 1) * tb] = value
-    for copy in pending + core_copies + y_copies + [c for row in z_copies for c in row]:
+    started = metric_copies + core_copies + y_copies
+    for row in copies + z_copies:
+        started += row
+    for copy in started:
         copy.wait_send()
 
 
@@ -228,16 +261,20 @@
     bf = jnp.bfloat16
     dma = pltpu.SemaphoreType.DMA
     vmem = pl.BlockSpec(memory_space=pltpu.VMEM)
+    whole = pl.BlockSpec(memory_space=pl.ANY)
     smem = pl.BlockSpec(memory_space=pltpu.SMEM)
     return pl.pallas_call(
         functools.partial(kernel, n, per_row, tb),
         out_shape=jax.ShapeDtypeStruct((tb, per_row * tb), jnp.float32),
-        in_specs=[smem, smem, smem, vmem, vmem, vmem],
+        in_specs=[smem, smem, smem, whole, whole, vmem],
         out_specs=vmem,
         scratch_shapes=[
+            pltpu.VMEM((basis, occ), bf),
+            pltpu.VMEM((slots, tb, tb), bf),
             pltpu.VMEM((tiles, occ, tb), bf),
-            pltpu.VMEM((occ, basis + occ), bf),
-            pltpu.VMEM((occ, basis + occ), bf),
+            pltpu.VMEM((CHUNKS, occ, basis // CHUNKS), bf),
+            pltpu.VMEM((CHUNKS, occ, basis // CHUNKS), bf),
+            pltpu.VMEM((occ, occ), bf),
             pltpu.VMEM((tiles, occ, tb), bf),
             pltpu.VMEM((tiles, tb, occ), bf),
             pltpu.VMEM((per_row, half_tiles, tb, tb), bf),
@@ -247,12 +284,13 @@
             pltpu.VMEM((per_row, z_count, tb, tb), bf),
             pltpu.VMEM((per_row, z_count - 1, tb, tb), bf),
             pltpu.VMEM((per_row, z_count - 1, tb, tb), bf),
-            dma, dma((n - 1,)), dma((n - 1,)),
+            dma((CHUNKS + 1,)), dma((CHUNKS,)), dma((n - 1,)), dma((n - 1,)),
+            dma((CHUNKS, n - 1)), dma((CHUNKS, n - 1)),
             dma((per_row,)), dma((per_row,)), dma((per_row,)), dma((per_row,)),
             dma((per_row, z_count - 1)), dma((per_row, z_count - 1)),
         ],
         compiler_params=pltpu.CompilerParams(
-            collective_id=0, has_side_effects=True, vmem_limit_bytes=48 * 1024 * 1024
+            collective_id=0, has_side_effects=True, vmem_limit_bytes=56 * 1024 * 1024
         ),
     )(slot, has, col_tiles.reshape(-1), three_center[0], orbitals, kron)
 

time: 62.9 us -> 62.3 us (level)
  other arithmetic: 0.19 us -> 1.9 us
  local copies, waits for them, and re-layouts: 5.27 us -> 3.87 us
  Pallas kernels: 57.1 us -> 56.3 us
    unnamed x12 -> x8, local copies, waits for them, and re-layouts: 5.02 us -> 3.14 us
    pallas_call x1, Pallas kernels: 57.1 us -> 56.3 us  [fused(): pl.pallas_call(functools.partial(kernel, n, per_row, tb), out_shape=jax.S...]
where the time goes in v2:
time: 62.3 us; the launch traced here: 62.1 us
  Pallas kernels  56.3 us (90%)
  local copies, waits for them, and re-layouts  3.87 us (6%)
  other arithmetic  1.9 us (3%)
    pallas_call x1, Pallas kernels, fused(): pl.pallas_call(functools.partial(kernel, n, per_row, tb), out_shape=jax.S...  56.3 us
    unnamed x8, local copies, waits for them, and re-layouts  3.14 us

profile of v2, /device:TPU:0, one launch (start us, length us, event | category | flops | bytes accessed | tf_op | source)
XLA Modules:
  0.0 62.1 jit_solution(16782926762382097711)
XLA Ops:
  0.0 0.0 copy-start.2
  0.0 0.7 %copy-done.2 = s32[1,16]{1,0:T(1,128)S(1)} copy-done((s32[1,16]{1,0:T(1,128)S(1)}, s32[1,16]{1,0:T(1,128)}, u32[]{:S(2)}) %copy-start.2) | copy-done | bytes 88
  0.7 0.1 fusion.1
  0.7 0.5 convert_element_type.5.has_ref
  1.3 0.7 %select_reduce_fusion.slot_ref = s32[64]{0:T(128)} fusion(s32[16]{0:T(128)S(1)} %bitcast.6), kind=kLoop, calls=%fused_computation.2 | loop fusion | flops 3008 | bytes 320 | tf_op jit(solution)/shard_map/reduce_sum | solution.py:253
  1.9 0.0 copy-start.1
  1.9 0.6 %copy-done.1 = bf16[1,16]{1,0:T(2,128)(2,1)S(1)} copy-done((bf16[1,16]{1,0:T(2,128)(2,1)S(1)}, bf16[1,16]{1,0:T(2,128)(2,1)}, u32[]{:S(2)}) %copy-start.1) | copy-done | bytes 56
  2.6 0.1 broadcast_in_dim.35
  2.7 0.1 broadcast_in_dim.36
  2.8 0.0 copy-start
  2.8 0.6 fusion.kron_ref
  3.4 0.1 copy-done
  3.5 0.1 copy.8
  3.5 0.6 reshape.13.col_ref
  4.1 56.3 %shard_map.55 = f32[128,512]{1,0:T(8,128)} custom-call(s32[64]{0:T(128)} %select_reduce_fusion.slot_ref, s32[64]{0:T(128)} %convert_element_type.5.has_ref, s32[64]{0:T(128)} %reshape.13.col_ref, bf16[16,128,128]{2,1,0:T(8,128)(2,1)} %bitcast.3, bf16[2048,256]{1,0:T(8,128)(2,1)} %orb_ref.1, bf16[16,256]{1,0:T(8,128)(2,1)} %fusion.kron_ref), custom_call_target="tpu_custom_call" | custom-call | tf_op jit(solution)/shard_map/pallas_call | solution.py:266
  60.4 1.7 %copy.10 = f32[128,512]{1,0:T(8,128)} copy(f32[128,512]{1,0:T(8,128)} %shard_map.55) | data formatting | bytes 524288
  (1 shorter events, 0.0 us)
Async XLA Ops:
  0.0 0.7 %copy-start.2 = (s32[1,16]{1,0:T(1,128)S(1)}, s32[1,16]{1,0:T(1,128)}, u32[]{:S(2)}) copy-start(s32[1,16]{1,0:T(1,128)} %param.6) | copy-start | bytes 196
  1.9 0.7 %copy-start.1 = (bf16[1,16]{1,0:T(2,128)(2,1)S(1)}, bf16[1,16]{1,0:T(2,128)(2,1)}, u32[]{:S(2)}) copy-start(bf16[1,16]{1,0:T(2,128)(2,1)} %param.9) | copy-start | bytes 100
  2.8 0.7 %copy-start = (s32[16,4]{0,1:T(4,128)S(1)}, s32[16,4]{0,1:T(4,128)}, u32[]{:S(2)}) copy-start(s32[16,4]{0,1:T(4,128)} %param.7) | copy-start | bytes 772

commit v3 on v2

--- a/solution.py
+++ b/solution.py
@@ -10,7 +10,8 @@
 MESH = pl.DeviceIdType.MESH
 Y_COUNT = 2
 CORES = 2
-CHUNKS = 4
+CHUNKS = 2
+HALVES = 2
 
 
 def general(three_center, pair_ids, col_tiles, orbitals, metric_root):
@@ -52,8 +53,8 @@
 
 def kernel(
     n, per_row, tb,
-    slot_ref, has_ref, col_ref, three_ref, orb_ref, kron_ref, out_ref,
-    orb_v, three_v, orb_t, send_h, recv_h, recv_m, fit_n, fit_t, send_c, recv_c, acc, send_y, recv_y, send_z, recv_z,
+    ids_ref, col_ref, three_ref, orb_ref, metric_ref, out_ref,
+    orb_v, three_v, orb_t, send_h, recv_h, send_m, recv_m, fit_n, fit_t, send_c, recv_c, acc, send_y, recv_y, send_z, recv_z,
     in_sem, own_sem, sm_sem, rm_sem, sh_sem, rh_sem, sc_sem, rc_sem, sy_sem, ry_sem, sz_sem, rz_sem,
 ):
     tiles = orb_ref.shape[0] // tb
@@ -106,21 +107,28 @@
             loads[b // chunk_tiles].wait()
         orb_t[b] = orb_v[b * tb:(b + 1) * tb, :].T
     loads[-1].wait()
-    pl.semaphore_wait(barrier, n - 1)
-
-    recv_m[rows_of(me), :] = kron_ref[...]
+    slots = three_v.shape[0]
+    ids = [ids_ref[0, i] for i in range(slots)]
+
+    def send_metric():
+        for k, off in enumerate(offsets):
+            copy = pltpu.make_async_remote_copy(
+                src_ref=send_m,
+                dst_ref=recv_m.at[rows_of(me), :],
+                send_sem=sm_sem.at[k],
+                recv_sem=rm_sem.at[k],
+                device_id={"fit": at(*off)},
+                device_id_type=MESH,
+            )
+            copy.start()
+            metric_copies.append(copy)
+
+    send_m[...] = jnp.zeros_like(send_m)
+    send_m[:, :n] = jnp.broadcast_to(metric_ref[...].astype(jnp.float32), (depth, n)).astype(
+        jnp.bfloat16
+    )
+    recv_m[rows_of(me), :] = send_m[...]
     metric_copies = []
-    for k, off in enumerate(offsets):
-        copy = pltpu.make_async_remote_copy(
-            src_ref=kron_ref,
-            dst_ref=recv_m.at[rows_of(me), :],
-            send_sem=sm_sem.at[k],
-            recv_sem=rm_sem.at[k],
-            device_id={"fit": at(*off)},
-            device_id_type=MESH,
-        )
-        copy.start()
-        metric_copies.append(copy)
 
     copies = []
     for c in range(chunks):
@@ -128,13 +136,18 @@
             total = jnp.zeros((occ, tb), jnp.float32)
             for r in range(per_row):
                 q = (c * chunk_tiles + t) * per_row + r
-                block = three_v[slot_ref[q]]
-                block = jnp.where(has_ref[q] > 0, block, jnp.zeros_like(block))
+                slot = jnp.int32(-1)
+                for i in range(slots):
+                    slot = jnp.where(ids[i] == q, i, slot)
+                block = three_v[jnp.maximum(slot, 0)]
+                block = jnp.where(slot >= 0, block, jnp.zeros_like(block))
                 total += lax.dot_general(
-                    orb_t[col_ref[q]], block, (((1,), (1,)), ((), ())),
+                    orb_t[col_ref[r, c * chunk_tiles + t]], block, (((1,), (1,)), ((), ())),
                     preferred_element_type=jnp.float32,
                 )
             send_h[c, :, t * tb:(t + 1) * tb] = total.astype(jnp.bfloat16)
+        if c == 0:
+            pl.semaphore_wait(barrier, n - 1)
         row = []
         for k, off in enumerate(offsets):
             dst = at(*off)
@@ -149,6 +162,8 @@
             copy.start()
             row.append(copy)
         copies.append(row)
+        if c == 0:
+            send_metric()
     owns = []
     for c in range(chunks):
         own = pltpu.make_async_copy(
@@ -158,7 +173,22 @@
         owns.append(own)
     for copy in metric_copies:
         copy.wait_recv()
-    kron = recv_m[...]
+    lanes = recv_m.shape[1]
+    wide = n * depth
+    expand = (
+        lax.broadcasted_iota(jnp.int32, (lanes, wide), 1) // depth
+        == lax.broadcasted_iota(jnp.int32, (lanes, wide), 0)
+    )
+    spread = jnp.dot(
+        recv_m[...],
+        jnp.where(expand, 1.0, 0.0).astype(jnp.bfloat16),
+        preferred_element_type=jnp.float32,
+    )
+    same = (
+        lax.broadcasted_iota(jnp.int32, (wide, wide), 1) % depth
+        == lax.broadcasted_iota(jnp.int32, (wide, wide), 0) % depth
+    )
+    kron = jnp.where(same, spread, 0.0).astype(jnp.bfloat16)
 
     for c in range(chunks):
         owns[c].wait()
@@ -176,8 +206,10 @@
 
     def part(a, r):
         return jnp.dot(
-            fit_t[a], fit_n[col_ref[a * per_row + r]], preferred_element_type=jnp.float32
-        )
+            fit_t[a], fit_n[col_ref[r, a]], preferred_element_type=jnp.float32
+        )
+
+    rows = tb // HALVES
 
     def to_core(r):
         for j in range(half_tiles):
@@ -195,14 +227,18 @@
         for j in range(quarter):
             t = j * Y_COUNT + (1 - y)
             value = part(t * CORES + core, r) + recv_c[r, t].astype(jnp.float32)
-            send_y[r, j] = value.astype(jnp.bfloat16)
-        copy = pltpu.make_async_remote_copy(
-            src_ref=send_y.at[r], dst_ref=recv_y.at[r],
-            send_sem=sy_sem.at[r], recv_sem=ry_sem.at[r],
-            device_id={"fit": at(0, 1, 0)}, device_id_type=MESH,
-        )
-        copy.start()
-        return copy
+            for h in range(HALVES):
+                send_y[r, h, j] = value[h * rows:(h + 1) * rows].astype(jnp.bfloat16)
+        out = []
+        for h in range(HALVES):
+            copy = pltpu.make_async_remote_copy(
+                src_ref=send_y.at[r, h], dst_ref=recv_y.at[r, h],
+                send_sem=sy_sem.at[r, h], recv_sem=ry_sem.at[r, h],
+                device_id={"fit": at(0, 1, 0)}, device_id_type=MESH,
+            )
+            copy.start()
+            out.append(copy)
+        return out
 
     core_copies = [to_core(0)]
     y_copies = []
@@ -216,27 +252,32 @@
             acc[r, j] = part(t * CORES + core, r) + recv_c[r, t].astype(jnp.float32)
     z_copies = []
     for r in range(per_row):
-        y_copies[r].wait_recv()
-        row = []
-        for k, dz in enumerate((2, 1, 3)):
-            zz = lax.rem(z + dz, z_count)
-            send_z[r, k] = (acc[r, zz] + recv_y[r, zz].astype(jnp.float32)).astype(jnp.bfloat16)
-            copy = pltpu.make_async_remote_copy(
-                src_ref=send_z.at[r, k], dst_ref=recv_z.at[r, k],
-                send_sem=sz_sem.at[r, k], recv_sem=rz_sem.at[r, k],
-                device_id={"fit": at(dz, 0, 0)}, device_id_type=MESH,
-            )
-            copy.start()
-            row.append(copy)
-        z_copies.append(row)
+        for h in range(HALVES):
+            span = pl.ds(h * rows, rows)
+            y_copies[r][h].wait_recv()
+            row = []
+            for k, dz in enumerate((2, 1, 3)):
+                zz = lax.rem(z + dz, z_count)
+                value = acc[r, zz, span, :] + recv_y[r, h, zz].astype(jnp.float32)
+                send_z[r, h, k] = value.astype(jnp.bfloat16)
+                copy = pltpu.make_async_remote_copy(
+                    src_ref=send_z.at[r, h, k], dst_ref=recv_z.at[r, h, k],
+                    send_sem=sz_sem.at[r, h, k], recv_sem=rz_sem.at[r, h, k],
+                    device_id={"fit": at(dz, 0, 0)}, device_id_type=MESH,
+                )
+                copy.start()
+                row.append(copy)
+            z_copies.append(row)
     for r in range(per_row):
-        value = acc[r, z] + recv_y[r, z].astype(jnp.float32)
-        for k in range(z_count - 1):
-            z_copies[r][k].wait_recv()
-            value += recv_z[r, k].astype(jnp.float32)
-        out_ref[:, r * tb:(r + 1) * tb] = value
-    started = metric_copies + core_copies + y_copies
-    for row in copies + z_copies:
+        for h in range(HALVES):
+            span = pl.ds(h * rows, rows)
+            value = acc[r, z, span, :] + recv_y[r, h, z].astype(jnp.float32)
+            for k in range(z_count - 1):
+                z_copies[r * HALVES + h][k].wait_recv()
+                value += recv_z[r, h, k].astype(jnp.float32)
+            out_ref[span, r * tb:(r + 1) * tb] = value
+    started = metric_copies + core_copies
+    for row in copies + y_copies + z_copies:
         started += row
     for copy in started:
         copy.wait_send()
@@ -247,15 +288,6 @@
     slots, tb = three_center.shape[1:3]
     basis, occ = orbitals.shape
     depth = occ // n
-    pairs = tiles * per_row
-    match = pair_ids[0][None, :] == jnp.arange(pairs, dtype=jnp.int32)[:, None]
-    has = jnp.any(match, axis=1).astype(jnp.int32)
-    slot = jnp.sum(jnp.where(match, jnp.arange(slots, dtype=jnp.int32)[None, :], 0), axis=1)
-    lane = jnp.arange(n * depth, dtype=jnp.int32)
-    spread = jnp.repeat(metric_root[0], depth)
-    kron = jnp.where(
-        (lane % depth)[None, :] == jnp.arange(depth, dtype=jnp.int32)[:, None], spread[None, :], 0
-    ).astype(jnp.bfloat16)
     z_count = n // (Y_COUNT * CORES)
     half_tiles = tiles // CORES
     bf = jnp.bfloat16
@@ -266,7 +298,7 @@
     return pl.pallas_call(
         functools.partial(kernel, n, per_row, tb),
         out_shape=jax.ShapeDtypeStruct((tb, per_row * tb), jnp.float32),
-        in_specs=[smem, smem, smem, whole, whole, vmem],
+        in_specs=[smem, smem, whole, whole, vmem],
         out_specs=vmem,
         scratch_shapes=[
             pltpu.VMEM((basis, occ), bf),
@@ -274,25 +306,26 @@
             pltpu.VMEM((tiles, occ, tb), bf),
             pltpu.VMEM((CHUNKS, occ, basis // CHUNKS), bf),
             pltpu.VMEM((CHUNKS, occ, basis // CHUNKS), bf),
-            pltpu.VMEM((occ, occ), bf),
+            pltpu.VMEM((depth, 128), bf),
+            pltpu.VMEM((occ, 128), bf),
             pltpu.VMEM((tiles, occ, tb), bf),
             pltpu.VMEM((tiles, tb, occ), bf),
             pltpu.VMEM((per_row, half_tiles, tb, tb), bf),
             pltpu.VMEM((per_row, half_tiles, tb, tb), bf),
             pltpu.VMEM((per_row, z_count, tb, tb), jnp.float32),
-            pltpu.VMEM((per_row, z_count, tb, tb), bf),
-            pltpu.VMEM((per_row, z_count, tb, tb), bf),
-            pltpu.VMEM((per_row, z_count - 1, tb, tb), bf),
-            pltpu.VMEM((per_row, z_count - 1, tb, tb), bf),
+            pltpu.VMEM((per_row, HALVES, z_count, tb // HALVES, tb), bf),
+            pltpu.VMEM((per_row, HALVES, z_count, tb // HALVES, tb), bf),
+            pltpu.VMEM((per_row, HALVES, z_count - 1, tb // HALVES, tb), bf),
+            pltpu.VMEM((per_row, HALVES, z_count - 1, tb // HALVES, tb), bf),
             dma((CHUNKS + 1,)), dma((CHUNKS,)), dma((n - 1,)), dma((n - 1,)),
             dma((CHUNKS, n - 1)), dma((CHUNKS, n - 1)),
-            dma((per_row,)), dma((per_row,)), dma((per_row,)), dma((per_row,)),
-            dma((per_row, z_count - 1)), dma((per_row, z_count - 1)),
+            dma((per_row,)), dma((per_row,)), dma((per_row, HALVES)), dma((per_row, HALVES)),
+            dma((per_row, HALVES, z_count - 1)), dma((per_row, HALVES, z_count - 1)),
         ],
         compiler_params=pltpu.CompilerParams(
             collective_id=0, has_side_effects=True, vmem_limit_bytes=56 * 1024 * 1024
         ),
-    )(slot, has, col_tiles.reshape(-1), three_center[0], orbitals, kron)
+    )(pair_ids, col_tiles.T, three_center[0], orbitals, metric_root)
 
 
 def solution(mesh):

time: 62.3 us -> 55.3 us (0.89)
  Pallas kernels: 56.3 us -> 53.4 us
  local copies, waits for them, and re-layouts: 3.87 us -> 1.67 us
  other arithmetic: 1.9 us -> 0 us
    pallas_call x1, Pallas kernels: 56.3 us -> 53.4 us  [fused(): pl.pallas_call(functools.partial(kernel, n, per_row, tb), out_shape=jax.S...]
    unnamed x8 -> x1, local copies, waits for them, and re-layouts: 3.14 us -> 1.67 us
    reduce_sum x1 -> x0, other arithmetic: 0.66 us -> none  [fused(): jnp.sum(jnp.where(match, jnp.arange(slots, dtype=jnp.int32)[None, :], 0),...]
where the time goes in v3:
time: 55.3 us; the launch traced here: 55.1 us
  Pallas kernels  53.4 us (97%)
  local copies, waits for them, and re-layouts  1.67 us (3%)
    pallas_call x1, Pallas kernels, fused(): pl.pallas_call(functools.partial(kernel, n, per_row, tb), out_shape=jax.S...  53.4 us
    unnamed x1, local copies, waits for them, and re-layouts  1.67 us

profile of v3, /device:TPU:0, one launch (start us, length us, event | category | flops | bytes accessed | tf_op | source)
XLA Modules:
  0.0 55.1 jit_solution(17281549875555612718)
XLA Ops:
  0.0 53.4 %shard_map.55 = f32[128,512]{1,0:T(8,128)} custom-call(s32[1,16]{1,0:T(1,128)} %ids_ref.1, s32[4,16]{1,0:T(4,128)} %bitcast.3, bf16[16,128,128]{2,1,0:T(8,128)(2,1)} %bitcast.2, bf16[2048,256]{1,0:T(8,128)(2,1)} %orb_ref.1, bf16[1,16]{1,0:T(2,128)(2,1)} %metric_ref.1), custom_call_target="tpu_custom_call" | custom-call | tf_op jit(solution)/shard_map/pallas_call | solution.py:298
  53.4 1.7 %copy.7 = f32[128,512]{1,0:T(8,128)} copy(f32[128,512]{1,0:T(8,128)} %shard_map.55) | data formatting | bytes 524288

commit v4 on v3

--- a/solution.py
+++ b/solution.py
@@ -10,7 +10,7 @@
 MESH = pl.DeviceIdType.MESH
 Y_COUNT = 2
 CORES = 2
-CHUNKS = 2
+CHUNKS = 4
 HALVES = 2
 
 
@@ -190,6 +190,52 @@
     )
     kron = jnp.where(same, spread, 0.0).astype(jnp.bfloat16)
 
+    half_tiles = tiles // CORES
+    quarter = half_tiles // Y_COUNT
+
+    def part(a, r):
+        other = a if r == 0 else col_ref[r, a]
+        return jnp.dot(fit_t[a], fit_n[other], preferred_element_type=jnp.float32)
+
+    rows = tb // HALVES
+
+    def to_core(r, c, lo, hi):
+        for j in range(lo, hi):
+            send_c[r, j] = part(j * CORES + (1 - core), r).astype(jnp.bfloat16)
+        copy = pltpu.make_async_remote_copy(
+            src_ref=send_c.at[r, lo:hi], dst_ref=recv_c.at[r, lo:hi],
+            send_sem=sc_sem.at[r, c], recv_sem=rc_sem.at[r, c],
+            device_id={"fit": at(0, 0, 1)}, device_id_type=MESH,
+        )
+        copy.start()
+        return copy
+
+    def to_y(r, c, lo, hi):
+        core_copies[r][c].wait_recv()
+        for j in range(lo, hi):
+            t = j * Y_COUNT + (1 - y)
+            value = part(t * CORES + core, r) + recv_c[r, t].astype(jnp.float32)
+            for h in range(HALVES):
+                send_y[r, h, j] = value[h * rows:(h + 1) * rows].astype(jnp.bfloat16)
+        out = []
+        for h in range(HALVES):
+            copy = pltpu.make_async_remote_copy(
+                src_ref=send_y.at[r, h, lo:hi], dst_ref=recv_y.at[r, h, lo:hi],
+                send_sem=sy_sem.at[r, c, h], recv_sem=ry_sem.at[r, c, h],
+                device_id={"fit": at(0, 1, 0)}, device_id_type=MESH,
+            )
+            copy.start()
+            out.append(copy)
+        return out
+
+    core_copies = [[]]
+    y_copies = [[]]
+    core_step = half_tiles // chunks
+    y_step = quarter // chunks
+
+    def first_to_y(c):
+        return to_y(0, c, c * y_step, (c + 1) * y_step)
+
     for c in range(chunks):
         owns[c].wait()
         for copy in copies[c]:
@@ -200,52 +246,17 @@
             ).astype(jnp.bfloat16)
             fit_n[c * chunk_tiles + t] = value
             fit_t[c * chunk_tiles + t] = value.T
-
-    half_tiles = tiles // CORES
-    quarter = half_tiles // Y_COUNT
-
-    def part(a, r):
-        return jnp.dot(
-            fit_t[a], fit_n[col_ref[r, a]], preferred_element_type=jnp.float32
-        )
-
-    rows = tb // HALVES
-
-    def to_core(r):
-        for j in range(half_tiles):
-            send_c[r, j] = part(j * CORES + (1 - core), r).astype(jnp.bfloat16)
-        copy = pltpu.make_async_remote_copy(
-            src_ref=send_c.at[r], dst_ref=recv_c.at[r],
-            send_sem=sc_sem.at[r], recv_sem=rc_sem.at[r],
-            device_id={"fit": at(0, 0, 1)}, device_id_type=MESH,
-        )
-        copy.start()
-        return copy
-
-    def to_y(r):
-        core_copies[r].wait_recv()
-        for j in range(quarter):
-            t = j * Y_COUNT + (1 - y)
-            value = part(t * CORES + core, r) + recv_c[r, t].astype(jnp.float32)
-            for h in range(HALVES):
-                send_y[r, h, j] = value[h * rows:(h + 1) * rows].astype(jnp.bfloat16)
-        out = []
-        for h in range(HALVES):
-            copy = pltpu.make_async_remote_copy(
-                src_ref=send_y.at[r, h], dst_ref=recv_y.at[r, h],
-                send_sem=sy_sem.at[r, h], recv_sem=ry_sem.at[r, h],
-                device_id={"fit": at(0, 1, 0)}, device_id_type=MESH,
-            )
-            copy.start()
-            out.append(copy)
-        return out
-
-    core_copies = [to_core(0)]
-    y_copies = []
+        core_copies[0].append(to_core(0, c, c * core_step, (c + 1) * core_step))
+        if c < chunks - 1:
+            y_copies[0].append(first_to_y(c))
+
     for r in range(1, per_row):
-        core_copies.append(to_core(r))
-        y_copies.append(to_y(r - 1))
-    y_copies.append(to_y(per_row - 1))
+        core_copies.append([to_core(r, 0, 0, half_tiles)])
+        if r == 1:
+            y_copies[0].append(first_to_y(chunks - 1))
+        else:
+            y_copies.append([to_y(r - 1, 0, 0, quarter)])
+    y_copies.append([to_y(per_row - 1, 0, 0, quarter)])
     for r in range(per_row):
         for j in range(quarter):
             t = j * Y_COUNT + y
@@ -254,7 +265,8 @@
     for r in range(per_row):
         for h in range(HALVES):
             span = pl.ds(h * rows, rows)
-            y_copies[r][h].wait_recv()
+            for group in y_copies[r]:
+                group[h].wait_recv()
             row = []
             for k, dz in enumerate((2, 1, 3)):
                 zz = lax.rem(z + dz, z_count)
@@ -276,9 +288,12 @@
                 z_copies[r * HALVES + h][k].wait_recv()
                 value += recv_z[r, h, k].astype(jnp.float32)
             out_ref[span, r * tb:(r + 1) * tb] = value
-    started = metric_copies + core_copies
-    for row in copies + y_copies + z_copies:
+    started = list(metric_copies)
+    for row in copies + core_copies + z_copies:
         started += row
+    for groups in y_copies:
+        for group in groups:
+            started += group
     for copy in started:
         copy.wait_send()
 
@@ -319,7 +334,8 @@
             pltpu.VMEM((per_row, HALVES, z_count - 1, tb // HALVES, tb), bf),
             dma((CHUNKS + 1,)), dma((CHUNKS,)), dma((n - 1,)), dma((n - 1,)),
             dma((CHUNKS, n - 1)), dma((CHUNKS, n - 1)),
-            dma((per_row,)), dma((per_row,)), dma((per_row, HALVES)), dma((per_row, HALVES)),
+            dma((per_row, CHUNKS)), dma((per_row, CHUNKS)),
+            dma((per_row, CHUNKS, HALVES)), dma((per_row, CHUNKS, HALVES)),
             dma((per_row, HALVES, z_count - 1)), dma((per_row, HALVES, z_count - 1)),
         ],
         compiler_params=pltpu.CompilerParams(

time: 55.3 us -> 55.4 us (level)
  no operation moved by 1% of the time
where the time goes in v4:
time: 55.4 us; the launch traced here: 55.2 us
  Pallas kernels  53.5 us (97%)
  local copies, waits for them, and re-layouts  1.67 us (3%)
    pallas_call x1, Pallas kernels, fused(): pl.pallas_call(functools.partial(kernel, n, per_row, tb), out_shape=jax.S...  53.5 us
    unnamed x1, local copies, waits for them, and re-layouts  1.67 us

profile of v4, /device:TPU:0, one launch (start us, length us, event | category | flops | bytes accessed | tf_op | source)
XLA Modules:
  0.0 55.2 jit_solution(5335503805923651692)
XLA Ops:
  0.0 53.5 %shard_map.55 = f32[128,512]{1,0:T(8,128)} custom-call(s32[1,16]{1,0:T(1,128)} %ids_ref.1, s32[4,16]{1,0:T(4,128)} %bitcast.3, bf16[16,128,128]{2,1,0:T(8,128)(2,1)} %bitcast.2, bf16[2048,256]{1,0:T(8,128)(2,1)} %orb_ref.1, bf16[1,16]{1,0:T(2,128)(2,1)} %metric_ref.1), custom_call_target="tpu_custom_call" | custom-call | tf_op jit(solution)/shard_map/pallas_call | solution.py:313
  53.5 1.7 %copy.7 = f32[128,512]{1,0:T(8,128)} copy(f32[128,512]{1,0:T(8,128)} %shard_map.55) | data formatting | bytes 524288
